TPU v7x, 32 devices: a whole 2x2x4 slice. The times are simulated.
32 devices in a mesh: row: 4 (over z), col: 8 (over y, x, core).
Axes of the slice: x: 2, y: 2, z: 4, core: 2. Of those that a mesh axis runs over, the one named last changes fastest.
Arguments:
- s_slab: bfloat16 [128, 262144], P(None, ('row', 'col')), may hold values from -4 to 4
- p_blocks: bfloat16 [4, 8, 64, 128, 128], P('row', 'col'), may hold values from -0.5 to 0.5
- p_index: int32 [4, 8, 2, 64], P('row', 'col'), may hold values from -1 to 2047, as said below
Outputs:
- purified: bfloat16 [128, 262144], P(None, ('row', 'col'))
Inputs may be any that keep to these rules, and one draw needn't show every extreme that they name: `p_index`: the slot on device (r, c) holds blocks whose block column lies in r * 512 to (r + 1) * 512 - 1 and whose block row k has (k // 64) % 8 == c; no block appears twice; live slots come first in each device's list and both entries of a slot are -1 or both are live; some device has all 64 slots live in every draw.
All inputs are finite; a program needn't handle non-finite values.
Results may differ from a plain program's by a relative error of at most 0.0034.
Values may be sent and summed in bfloat16 or wider, within the bound.
No kernel may reach another device: no remote copies, remote signals or barrier semaphores. Data moves between devices by JAX's collectives and lax.ppermute only.
A program may use at most 192 MiB of HBM per device.

v0:
```python
import jax
import jax.numpy as jnp
from jax import lax
from jax.experimental import pallas as pl
from jax.experimental.pallas import tpu as pltpu
from jax.sharding import PartitionSpec as P

LEVELS = ((28, 16, 14), (28, 18, 14), (28, 20, 16), (32, 24, 20))
PARTS = (32, 32, 32, 32)
SHIFT = 1024
COST = 1 << 16
HIDE = 30_000_000_000


def smem():
    return pl.BlockSpec(memory_space=pltpu.SMEM)


def anywhere():
    return pl.BlockSpec(memory_space=pl.ANY)


def vmem():
    return pl.BlockSpec(memory_space=pltpu.VMEM)


def pairs(n, t):
    return [(i, i ^ t) for i in range(n)]


def number(index, per_piece, owner_of, n_owner, wide):
    slots = index.shape[1]
    f32 = jnp.float32
    lane = lax.broadcasted_iota(jnp.int32, (slots, slots), 1)
    sub = lax.broadcasted_iota(jnp.int32, (slots, slots), 0)
    key_r = index.astype(f32)
    key_c = jnp.sum(jnp.where(lane == sub, key_r, 0.0), axis=1, keepdims=True)
    index_c = jnp.maximum(key_c.astype(jnp.int32), 0)
    owner_r = owner_of(jnp.maximum(index, 0)).astype(f32)
    owner_c = owner_of(index_c).astype(f32)
    local_c = lax.rem(index_c, per_piece).astype(f32)
    same = jnp.where(key_c == key_r, 1.0, 0.0)
    before = jnp.where(lane < sub, 1.0, 0.0)
    after = jnp.where(sub < lane, 1.0, 0.0)
    kin = jnp.where(owner_c == owner_r, 1.0, 0.0)
    first_c = jnp.where(jnp.sum(same * before, axis=1, keepdims=True) == 0.0, 1.0, 0.0)
    first_c = jnp.where(key_c >= 0.0, first_c, 0.0)
    first_r = jnp.where(jnp.sum(same * after, axis=0, keepdims=True) == 0.0, 1.0, 0.0)
    first_r = jnp.where(key_r >= 0.0, first_r, 0.0)
    rank_c = jnp.sum(kin * before * first_r, axis=1, keepdims=True)
    rank_r = jnp.sum(same * (first_c * rank_c), axis=0, keepdims=True)
    lanes = lax.broadcasted_iota(jnp.int32, (slots, wide), 1).astype(f32)
    spot = jnp.where(lanes == rank_c + 1.0, local_c, 0.0) + jnp.where(lanes == 0.0, 1.0, 0.0)
    rows = []
    for owner in range(n_owner):
        mine = first_c * jnp.where(owner_c == float(owner), 1.0, 0.0)
        rows.append(jnp.sum(spot * mine, axis=0, keepdims=True))
    return owner_r.astype(jnp.int32), rank_r.astype(jnp.int32), first_r, rows


def ask_kernel(n_row, n_col, per_piece, levels, index, line, places):
    wide = line.shape[1]
    k, j = index[0, 0, 0:1, :], index[0, 0, 1:2, :]
    from_r, from_rank, _, asks = number(
        k, per_piece, lambda v: lax.div(v, per_piece * n_col), n_row, wide
    )
    to_r, to_rank, first, lists = number(
        j, per_piece, lambda v: lax.rem(lax.div(v, per_piece), n_col), n_col, wide
    )
    row = lax.axis_index("row")
    need = jnp.zeros((1, 1), jnp.float32)
    for near, far, col in levels:
        over = jnp.zeros((1, 1), jnp.float32)
        for owner, ask in enumerate(asks):
            cap = jnp.where((owner ^ row) <= 1, float(near), float(far))
            over = jnp.maximum(over, jnp.where(ask[:, 0:1] > cap, 1.0, 0.0))
        for item in lists:
            over = jnp.maximum(over, jnp.where(item[:, 0:1] > float(col), 1.0, 0.0))
        need = need + over
    lane = lax.broadcasted_iota(jnp.int32, (1, wide), 1)
    told = jnp.concatenate(lists, axis=0) * float(SHIFT)
    for owner, ask in enumerate(asks):
        values = jnp.where(lane == wide - 1, need, ask + told)
        line[owner * n_col : (owner + 1) * n_col, :] = values.astype(jnp.int32)
    alive = jnp.where(j >= 0, 1.0, 0.0)
    live = jnp.sum(alive, axis=1, keepdims=True)
    places[0:1, :] = from_r ^ row
    places[1:2, :] = from_rank
    places[2:3, :] = to_r
    places[3:4, :] = to_rank
    places[4:5, :] = first.astype(jnp.int32)
    places[5:6, :] = jnp.broadcast_to(live, j.shape).astype(jnp.int32)


def fetch(copies):
    for copy in copies:
        copy.start()
    for copy in copies:
        copy.wait()


def pack_kernel(n_row, n_col, blk, spans, heard, slab, *refs):
    packs, (asks, sems) = refs[: n_row * len(spans)], refs[n_row * len(spans) :]
    row, col = lax.axis_index("row"), lax.axis_index("col")
    fetch(
        [
            pltpu.make_async_copy(heard.at[(row ^ t) * n_col + col], asks.at[t], sems.at[t])
            for t in range(n_row)
        ]
    )
    for p, (first, rows) in enumerate(spans):
        for t in range(n_row):
            pack = packs[p * n_row + t]

            def copy(i, carry):
                at = pl.multiple_of((asks[t, 0, 1 + i] & (SHIFT - 1)) * blk, blk)
                pack[i] = slab[first : first + rows, pl.ds(at, blk)]
                return carry

            lax.fori_loop(0, asks[t, 0, 0] & (SHIFT - 1), copy, 0)


def product_kernel(n_row, base, group, places, stored, *refs):
    panels = refs[:n_row]
    sums, held, total = refs[-3:]
    n_col, cap = sums.shape[:2]
    for t, panel in enumerate(panels):
        held[base[t] : base[t] + panel.shape[0]] = panel[...]
    live = places[5, 0]

    def start(t):
        at = jnp.int32(base[0])
        for i in range(1, n_row):
            at = jnp.where(t == i, base[i], at)
        return at

    def step(g, carry):
        products = []
        for u in range(group):
            s = g * group + u
            here = start(places[0, s]) + places[1, s]
            products.append(jnp.dot(held[here], stored[s], preferred_element_type=jnp.float32))
        for u in range(group):
            s = g * group + u
            o = jnp.where(s < live, places[2, s] * cap + places[3, s], n_col * cap)
            total[o] = jnp.where(places[4, s] == 1, 0.0, total[o]) + products[u]
        return carry

    lax.fori_loop(0, lax.div(live + group - 1, group), step, 0)
    for t in range(n_col):
        sums[t] = total[t * cap : (t + 1) * cap].astype(jnp.bfloat16)


def combine_kernel(blk, first, chunks, lists, slab, sums, *refs):
    out, total, ready, sems = refs[-4:]
    n_col = sums.shape[0]
    pieces, rows = total.shape[:2]
    for i in range(pieces):
        total[i] = 3.0 * slab[first : first + rows, i * blk : (i + 1) * blk].astype(jnp.float32)
    for t in range(n_col):

        def add(i, carry):
            total[lists[t, 1 + i] >> 10] -= 2.0 * sums[t, i].astype(jnp.float32)
            return carry

        lax.fori_loop(0, lists[t, 0] >> 10, add, 0)
    each = pieces // chunks
    copies = []
    for q in range(chunks):
        for i in range(q * each, (q + 1) * each):
            ready[:, i * blk : (i + 1) * blk] = total[i].astype(ready.dtype)
        here = pl.ds(q * each * blk, each * blk)
        copies.append(
            pltpu.make_async_copy(ready.at[:, here], out.at[pl.ds(first, rows), here], sems.at[q])
        )
        copies[-1].start()
    for copy in copies:
        copy.wait()


def exchange(heard, lists, places, s_slab, stored, caps_in, cap, parts):
    blk = s_slab.shape[0]
    width = s_slab.shape[1]
    n_row = lax.axis_size("row")
    n_col = lax.axis_size("col")
    slots = stored.shape[0]
    pieces = width // blk
    group = 8 if slots % 8 == 0 else 1
    chunks = 4 if pieces % 4 == 0 else 1
    base = [sum(caps_in[:t]) for t in range(n_row)]
    tight = sum(caps_in) <= 2 * slots
    params = pltpu.CompilerParams(vmem_limit_bytes=(16 if tight else 48) * 1024 * 1024)
    cost = pl.CostEstimate(flops=0, bytes_accessed=COST, transcendentals=0)
    spans = [(sum(parts[:i]), rows) for i, rows in enumerate(parts)]

    def pack(some):
        done = pl.pallas_call(
            lambda *refs: pack_kernel(n_row, n_col, blk, some, *refs),
            out_shape=[
                jax.ShapeDtypeStruct((c, rows, blk), jnp.bfloat16)
                for first, rows in some
                for c in caps_in
            ],
            in_specs=[anywhere(), vmem()],
            out_specs=[vmem()] * (n_row * len(some)),
            scratch_shapes=[
                pltpu.SMEM((n_row,) + heard.shape[1:], jnp.int32),
                pltpu.SemaphoreType.DMA((n_row,)),
            ],
            compiler_params=params,
            cost_estimate=cost,
            name="pack",
        )(heard, s_slab)
        return [done[i * n_row : (i + 1) * n_row] for i in range(len(some))]

    packed = pack(spans[:1])
    if len(spans) > 1:
        packed += pack(spans[1:])
        places, packed[1:] = lax.optimization_barrier((places, packed[1:]))
    result = None
    for (first, rows), packs in zip(spans, packed):
        panels = [packs[0]] + [
            lax.ppermute(packs[t], "row", pairs(n_row, t)) for t in range(1, n_row)
        ]
        sums = pl.pallas_call(
            lambda *refs: product_kernel(n_row, base, group, *refs),
            out_shape=jax.ShapeDtypeStruct((n_col, cap, rows, blk), jnp.bfloat16),
            in_specs=[smem()] + [vmem()] * (1 + n_row),
            out_specs=vmem(),
            scratch_shapes=[
                pltpu.VMEM((sum(caps_in), rows, blk), jnp.bfloat16),
                pltpu.VMEM((n_col * cap + 1, rows, blk), jnp.float32),
            ],
            compiler_params=params,
            cost_estimate=pl.CostEstimate(flops=HIDE, bytes_accessed=COST, transcendentals=0),
            name="product",
        )(places, stored, *panels)
        sums = lax.all_to_all(sums, "col", 0, 0, tiled=True)
        extra = [] if result is None else [result]
        result = pl.pallas_call(
            lambda *refs, first=first: combine_kernel(blk, first, chunks, *refs),
            out_shape=jax.ShapeDtypeStruct(s_slab.shape, s_slab.dtype),
            in_specs=[smem(), vmem(), vmem()] + [anywhere()] * len(extra),
            out_specs=anywhere(),
            scratch_shapes=[
                pltpu.VMEM((pieces, rows, blk), jnp.float32),
                pltpu.VMEM((rows, width), jnp.bfloat16),
                pltpu.SemaphoreType.DMA((chunks,)),
            ],
            input_output_aliases={3: 0} if extra else {},
            compiler_params=params,
            cost_estimate=cost,
            name="combine",
        )(lists, s_slab, sums, *extra)
    return result


def body(s_slab, p_blocks, p_index):
    blk = s_slab.shape[0]
    per_piece = s_slab.shape[1] // blk
    n_row = lax.axis_size("row")
    n_col = lax.axis_size("col")
    slots = p_blocks.shape[2]
    stored = p_blocks[0, 0]
    full = min(per_piece, slots)
    wide = -(-(2 + full) // 128) * 128
    parts = PARTS if sum(PARTS) == blk else (blk,)
    levels = [level for level in LEVELS if max(level) < full]
    levels.append((full, full, full))

    line, places = pl.pallas_call(
        lambda *refs: ask_kernel(n_row, n_col, per_piece, levels[:-1], *refs),
        out_shape=[
            jax.ShapeDtypeStruct((n_row * n_col, wide), jnp.int32),
            jax.ShapeDtypeStruct((6, slots), jnp.int32),
        ],
        name="ask",
    )(p_index)
    heard = lax.all_to_all(line, ("row", "col"), 0, 0, tiled=True)
    lines = heard.reshape(n_row * n_col, 1, wide)
    lists = heard.reshape(n_row, n_col, wide)[lax.axis_index("row")]

    def run(level):
        near, far, cap = level
        caps_in = [near, near] + [far] * (n_row - 2)
        return lambda: exchange(lines, lists, places, s_slab, stored, caps_in, cap, parts)

    if len(levels) == 1:
        return run(levels[0])()
    return lax.switch(jnp.max(heard[:, wide - 1]), [run(level) for level in levels])


def solution(mesh):
    placed = (
        P(None, ("row", "col")),
        P("row", "col", None, None, None),
        P("row", "col", None, None),
    )
    return jax.shard_map(
        body, mesh=mesh, in_specs=placed, out_specs=P(None, ("row", "col")), check_vma=False
    )
```

profile of v0, /device:TPU:0, one launch (start us, length us, event | category | flops | bytes accessed | tf_op | source)
XLA Modules:
  0.0 129.2 jit_solution(17442294104998986580)
XLA Ops:
  1.7 7.3 %all-to-all-start.20 = ((s32[32,1,128]{2,1,0:T(1,128)}), s32[32,1,128]{2,1,0:T(1,128)S(1)}, u32[]{:S(2)}, u32[]{:S(2)}) async-start(s32[32,1,128]{2,1,0:T(1,128)} %bitcast.40), calls=%async_computation.20 | async-start | bytes 32768 | tf_op jit(solution)/shard_map/all_to_all | solution.py:279
  9.0 7.1 %all-to-all-done.20 = s32[32,1,128]{2,1,0:T(1,128)S(1)} async-done(((s32[32,1,128]{2,1,0:T(1,128)}), s32[32,1,128]{2,1,0:T(1,128)S(1)}, u32[]{:S(2)}, u32[]{:S(2)}) %all-to-all-start.20) | async-done | bytes 16416 | tf_op jit(solution)/shard_map/all_to_all | solution.py:279
  17.4 111.6 %conditional.1 = (bf16[128,8192]{1,0:T(8,128)(2,1)}) conditional(s32[]{:T(128)} %clamp.3, (s32[32,1,128]{2,1,0:T(1,128)S(1)}, bf16[128,8192]{1,0:T(8,128)(2,1)}, s32[6,64]{1,0:T(8,128)S(1)}, bf16[1,1,64,128,128]{4,3,2,1,0:T(8,128)(2,1)}, s32[32,1,128]{2,1,0:T(1,128)S(1)}, /*index=5*/s32[]{:T(128)}, s32[]{:T(128)}, ...), branch_computations={%region_1.0_spmd, %region_2.0_spmd, %region_3.0_spmd, %region_4.0_... | conditional | flops 120000004096 | bytes 105521944 | solution.py:290
  17.4 2.9 %pack.15 = (bf16[28,32,128]{2,1,0:T(8,128)(2,1)S(1)}, bf16[28,32,128]{2,1,0:T(8,128)(2,1)S(1)}, bf16[20,32,128]{2,1,0:T(8,128)(2,1)S(1)}, bf16[20,32,128]{2,1,0:T(8,128)(2,1)S(1)}) custom-call(s32[32,1,128]{2,1,0:T(1,128)S(1)} %get-tuple-element.402, bf16[128,8192]{1,0:T(8,128)(2,1)} %get-tuple-element.253.refs_1_), custom_call_target="tpu_custom_call" | custom-call | bytes 65536 | tf_op jit(solution)/shard_map/cond/branch_2_fun/pack/pallas_call | solution.py:197
  21.5 3.3 %collective-permute-start.35 = (bf16[20,32,128]{2,1,0:T(8,128)(2,1)S(1)}, bf16[20,32,128]{2,1,0:T(8,128)(2,1)S(1)}, u32[]{:S(2)}, u32[]{:S(2)}) collective-permute-start(bf16[20,32,128]{2,1,0:T(8,128)(2,1)S(1)} %get-tuple-element.162), channel_id=1, source_target_pairs={{0,24},{8,16},{16,8},{24,0},{1,25},{9,17},{17,9},{25,1},{2,26},{10... | collective-permute-start | bytes 491528 | tf_op jit(solution)/shard_map/cond/branch_2_fun/ppermute | solution.py:223
  24.8 3.1 %pack.14 = (bf16[28,32,128]{2,1,0:T(8,128)(2,1)S(1)}, bf16[28,32,128]{2,1,0:T(8,128)(2,1)S(1)}, bf16[20,32,128]{2,1,0:T(8,128)(2,1)}, bf16[20,32,128]{2,1,0:T(8,...) custom-call(s32[32,1,128]{2,1,0:T(1,128)S(1)} %get-tuple-element.402, ...), custom_call_target="tpu_custom_call" | custom-call | bytes 65536 | tf_op jit(solution)/shard_map/cond/branch_2_fun/pack/pallas_call | solution.py:197
  29.5 6.4 %collective-permute-done.34.refs_4_ = bf16[20,32,128]{2,1,0:T(8,128)(2,1)S(1)} collective-permute-done((bf16[20,32,128]{2,1,0:T(8,128)(2,1)S(1)}, bf16[20,32,128]{2,1,0:T(8,128)(2,1)S(1)}, u32[]{:S(2)}, u32[]{:S(2)}) %collective-permute-start.34) | collective-permute-done | bytes 163872 | tf_op jit(solution)/shard_map/cond/branch_2_fun/ppermute | solution.py:223
  36.7 4.5 %collective-permute-start.27 = (bf16[28,32,128]{2,1,0:T(8,128)(2,1)S(1)}, bf16[28,32,128]{2,1,0:T(8,128)(2,1)S(1)}, u32[]{:S(2)}, u32[]{:S(2)}) collective-permute-start(bf16[28,32,128]{2,1,0:T(8,128)(2,1)S(1)} %get-tuple-element.152), channel_id=1, source_target_pairs={{0,8},{8,0},{16,24},{24,16},{1,9},{9,1},{17,25},{25,17},{2,10},{10... | collective-permute-start | bytes 688136 | tf_op jit(solution)/shard_map/cond/branch_2_fun/ppermute | solution.py:223
  41.3 2.9 %product.31 = bf16[8,16,32,128]{3,2,1,0:T(8,128)(2,1)} custom-call(s32[6,64]{1,0:T(8,128)S(1)} %get-tuple-element.145.refs_0_, bf16[64,128,128]{2,1,0:T(8,128)(2,1)S(1)} %bitcast.52, bf16[28,32,128]{2,1,0:T(8,128)(2,1)S(1)} %get-tuple-element.159.refs_2_, bf16[28,32,128]{2,1,0:T(8,128)(2,1)S(1)} %collective-permute-done.33.refs_3_, ...), custom_call_target="tpu_custom_call" | custom-call | flops 30000001024 | bytes 65536 | tf_op jit(solution)/shard_map/cond/branch_2_fun/product/pallas_call | solution.py:225
  44.2 3.6 %all-to-all-start.11 = ((bf16[8,16,32,128]{3,2,1,0:T(8,128)(2,1)}), bf16[8,16,32,128]{3,2,1,0:T(8,128)(2,1)S(1)}, u32[]{:S(2)}, u32[]{:S(2)}) async-start(bf16[8,16,32,128]{3,2,1,0:T(8,128)(2,1)} %product.31), calls=%async_computation.11 | async-start | bytes 2097152 | tf_op jit(solution)/shard_map/cond/branch_2_fun/all_to_all | solution.py:238
  47.7 2.4 %collective-permute-done.31.refs_4_ = bf16[20,32,128]{2,1,0:T(8,128)(2,1)} collective-permute-done((bf16[20,32,128]{2,1,0:T(8,128)(2,1)}, bf16[20,32,128]{2,1,0:T(8,128)(2,1)}, u32[]{:S(2)}, u32[]{:S(2)}) %collective-permute-start.31) | collective-permute-done | bytes 163872 | tf_op jit(solution)/shard_map/cond/branch_2_fun/ppermute | solution.py:223
  51.7 9.5 %collective-permute-start.24 = (bf16[28,32,128]{2,1,0:T(8,128)(2,1)S(1)}, bf16[28,32,128]{2,1,0:T(8,128)(2,1)S(1)}, u32[]{:S(2)}, u32[]{:S(2)}) collective-permute-start(bf16[28,32,128]{2,1,0:T(8,128)(2,1)S(1)} %get-tuple-element.148), channel_id=1, source_target_pairs={{0,8},{8,0},{16,24},{24,16},{1,9},{9,1},{17,25},{25,17},{2,10},{10... | collective-permute-start | bytes 688136 | tf_op jit(solution)/shard_map/cond/branch_2_fun/ppermute | solution.py:223
  61.2 4.0 %product.30 = bf16[8,16,32,128]{3,2,1,0:T(8,128)(2,1)} custom-call(s32[6,64]{1,0:T(8,128)S(1)} %get-tuple-element.145.refs_0_, bf16[64,128,128]{2,1,0:T(8,128)(2,1)} %bitcast.49, bf16[28,32,128]{2,1,0:T(8,128)(2,1)S(1)} %get-tuple-element.155.refs_2_, bf16[28,32,128]{2,1,0:T(8,128)(2,1)S(1)} %collective-permute-done.30.refs_3_, ...), custom_call_target="tpu_custom_call" | custom-call | flops 30000001024 | bytes 65536 | tf_op jit(solution)/shard_map/cond/branch_2_fun/product/pallas_call | solution.py:225
  66.0 2.0 %collective-permute-start.26 = (bf16[20,32,128]{2,1,0:T(8,128)(2,1)S(1)}, bf16[20,32,128]{2,1,0:T(8,128)(2,1)S(1)}, u32[]{:S(2)}, u32[]{:S(2)}) collective-permute-start(bf16[20,32,128]{2,1,0:T(8,128)(2,1)S(1)} %get-tuple-element.150), channel_id=1, source_target_pairs={{0,24},{8,16},{16,8},{24,0},{1,25},{9,17},{17,9},{25,1},{2,26},{10... | collective-permute-start | bytes 491528 | tf_op jit(solution)/shard_map/cond/branch_2_fun/ppermute | solution.py:223
  69.0 3.6 %all-to-all-start.10 = ((bf16[8,16,32,128]{3,2,1,0:T(8,128)(2,1)}), bf16[8,16,32,128]{3,2,1,0:T(8,128)(2,1)S(1)}, u32[]{:S(2)}, u32[]{:S(2)}) async-start(bf16[8,16,32,128]{3,2,1,0:T(8,128)(2,1)} %product.30), calls=%async_computation.10 | async-start | bytes 2097152 | tf_op jit(solution)/shard_map/cond/branch_2_fun/all_to_all | solution.py:238
  72.6 4.0 %product.29 = bf16[8,16,32,128]{3,2,1,0:T(8,128)(2,1)} custom-call(s32[6,64]{1,0:T(8,128)S(1)} %get-tuple-element.145.refs_0_, bf16[64,128,128]{2,1,0:T(8,128)(2,1)} %bitcast.50, bf16[28,32,128]{2,1,0:T(8,128)(2,1)S(1)} %get-tuple-element.151.refs_2_, bf16[28,32,128]{2,1,0:T(8,128)(2,1)S(1)} %collective-permute-done.27.refs_3_, ...), custom_call_target="tpu_custom_call" | custom-call | flops 30000001024 | bytes 65536 | tf_op jit(solution)/shard_map/cond/branch_2_fun/product/pallas_call | solution.py:225
  76.5 11.4 %all-to-all-done.10.refs_2_ = bf16[8,16,32,128]{3,2,1,0:T(8,128)(2,1)S(1)} async-done(((bf16[8,16,32,128]{3,2,1,0:T(8,128)(2,1)}), bf16[8,16,32,128]{3,2,1,0:T(8,128)(2,1)S(1)}, u32[]{:S(2)}, u32[]{:S(2)}) %all-to-all-start.10) | async-done | bytes 1048608 | tf_op jit(solution)/shard_map/cond/branch_2_fun/all_to_all | solution.py:238
  87.9 3.6 %all-to-all-start.9 = ((bf16[8,16,32,128]{3,2,1,0:T(8,128)(2,1)}), bf16[8,16,32,128]{3,2,1,0:T(8,128)(2,1)S(1)}, u32[]{:S(2)}, u32[]{:S(2)}) async-start(bf16[8,16,32,128]{3,2,1,0:T(8,128)(2,1)} %product.29), calls=%async_computation.9 | async-start | bytes 2097152 | tf_op jit(solution)/shard_map/cond/branch_2_fun/all_to_all | solution.py:238
  91.5 2.9 %product.28 = bf16[8,16,32,128]{3,2,1,0:T(8,128)(2,1)S(1)} custom-call(s32[6,64]{1,0:T(8,128)S(1)} %get-tuple-element.145.refs_0_, bf16[64,128,128]{2,1,0:T(8,128)(2,1)} %bitcast.51, bf16[28,32,128]{2,1,0:T(8,128)(2,1)S(1)} %get-tuple-element.147.refs_2_, bf16[28,32,128]{2,1,0:T(8,128)(2,1)S(1)} %collective-permute-done.24.refs_3_, ...), custom_call_target="tpu_custom_call" | custom-call | flops 30000001024 | bytes 65536 | tf_op jit(solution)/shard_map/cond/branch_2_fun/product/pallas_call | solution.py:225
  95.4 11.4 %all-to-all-done.9.refs_2_ = bf16[8,16,32,128]{3,2,1,0:T(8,128)(2,1)S(1)} async-done(((bf16[8,16,32,128]{3,2,1,0:T(8,128)(2,1)}), bf16[8,16,32,128]{3,2,1,0:T(8,128)(2,1)S(1)}, u32[]{:S(2)}, u32[]{:S(2)}) %all-to-all-start.9) | async-done | bytes 1048608 | tf_op jit(solution)/shard_map/cond/branch_2_fun/all_to_all | solution.py:238
  106.8 3.6 %all-to-all-start.8 = ((bf16[8,16,32,128]{3,2,1,0:T(8,128)(2,1)}), bf16[8,16,32,128]{3,2,1,0:T(8,128)(2,1)S(1)}, u32[]{:S(2)}, u32[]{:S(2)}) async-start(bf16[8,16,32,128]{3,2,1,0:T(8,128)(2,1)} %copy-done.10), calls=%async_computation.8 | async-start | bytes 2097152 | tf_op jit(solution)/shard_map/cond/branch_2_fun/all_to_all | solution.py:238
  111.6 3.0 %combine.28.refs_3_ = bf16[128,8192]{1,0:T(8,128)(2,1)} custom-call(s32[8,128]{1,0:T(8,128)S(1)} %dynamic-slice_bitcast_fusion.2.refs_0_, bf16[128,8192]{1,0:T(8,128)(2,1)} %get-tuple-element.253.refs_1_, bf16[8,16,32,128]{3,2,1,0:T(8,128)(2,1)S(1)} %copy-done.3), custom_call_target="tpu_custom_call" | custom-call | bytes 65536 | tf_op jit(solution)/shard_map/cond/branch_2_fun/combine/pallas_call | solution.py:240
  118.5 7.2 %all-to-all-done.8.refs_2_ = bf16[8,16,32,128]{3,2,1,0:T(8,128)(2,1)S(1)} async-done(((bf16[8,16,32,128]{3,2,1,0:T(8,128)(2,1)}), bf16[8,16,32,128]{3,2,1,0:T(8,128)(2,1)S(1)}, u32[]{:S(2)}, u32[]{:S(2)}) %all-to-all-start.8) | async-done | bytes 1048608 | tf_op jit(solution)/shard_map/cond/branch_2_fun/all_to_all | solution.py:238
  125.7 2.9 %combine.31 = bf16[128,8192]{1,0:T(8,128)(2,1)} custom-call(s32[8,128]{1,0:T(8,128)S(1)} %dynamic-slice_bitcast_fusion.2.refs_0_, bf16[128,8192]{1,0:T(8,128)(2,1)} %get-tuple-element.253.refs_1_, bf16[8,16,32,128]{3,2,1,0:T(8,128)(2,1)S(1)} %all-to-all-done.8.refs_2_, bf16[128,8192]{1,0:T(8,128)(2,1)} %combine.30.refs_3_), custom_call_target="tpu_custom_call", output_to_operand_aliasing={{}: (3, {})} | custom-call | bytes 65536 | tf_op jit(solution)/shard_map/cond/branch_2_fun/combine/pallas_call | solution.py:240
  (38 shorter events, 15.4 us)
Async XLA Ops:
  1.7 14.4 %all-to-all-start.20 = ((s32[32,1,128]{2,1,0:T(1,128)}), s32[32,1,128]{2,1,0:T(1,128)S(1)}, u32[]{:S(2)}, u32[]{:S(2)}) async-start(s32[32,1,128]{2,1,0:T(1,128)} %bitcast.40), calls=%async_computation.20 | async-start | bytes 32768 | tf_op jit(solution)/shard_map/all_to_all | solution.py:279
  17.4 7.4 %copy-start.22 = (bf16[128,8192]{1,0:T(8,128)(2,1)S(1)}, bf16[128,8192]{1,0:T(8,128)(2,1)}, u32[]{:S(2)}) copy-start(bf16[128,8192]{1,0:T(8,128)(2,1)} %get-tuple-element.253.refs_1_) | copy-start | bytes 6291460 | tf_op jit(solution)/shard_map/cond
  17.4 23.9 %copy-start.29 = (bf16[1,1,64,128,128]{4,3,2,1,0:T(8,128)(2,1)S(1)}, bf16[1,1,64,128,128]{4,3,2,1,0:T(8,128)(2,1)}, u32[]{:S(2)}) copy-start(bf16[1,1,64,128,128]{4,3,2,1,0:T(8,128)(2,1)} %get-tuple-element.278) | copy-start | bytes 6291460 | tf_op jit(solution)/shard_map/cond
  20.4 20.9 %collective-permute-start.33 = (bf16[28,32,128]{2,1,0:T(8,128)(2,1)S(1)}, bf16[28,32,128]{2,1,0:T(8,128)(2,1)S(1)}, u32[]{:S(2)}, u32[]{:S(2)}) collective-permute-start(bf16[28,32,128]{2,1,0:T(8,128)(2,1)S(1)} %get-tuple-element.160), channel_id=1, source_target_pairs={{0,8},{8,0},{16,24},{24,16},{1,9},{9,1},{17,25},{25,17},{2,10},{10... | collective-permute-start | bytes 688136 | tf_op jit(solution)/shard_map/cond/branch_2_fun/ppermute | solution.py:223
  20.8 15.0 %collective-permute-start.34 = (bf16[20,32,128]{2,1,0:T(8,128)(2,1)S(1)}, bf16[20,32,128]{2,1,0:T(8,128)(2,1)S(1)}, u32[]{:S(2)}, u32[]{:S(2)}) collective-permute-start(bf16[20,32,128]{2,1,0:T(8,128)(2,1)S(1)} %get-tuple-element.161), channel_id=1, source_target_pairs={{0,16},{8,24},{16,0},{24,8},{1,17},{9,25},{17,1},{25,9},{2,18},{10... | collective-permute-start | bytes 491528 | tf_op jit(solution)/shard_map/cond/branch_2_fun/ppermute | solution.py:223
  21.5 15.2 %collective-permute-start.35 = (bf16[20,32,128]{2,1,0:T(8,128)(2,1)S(1)}, bf16[20,32,128]{2,1,0:T(8,128)(2,1)S(1)}, u32[]{:S(2)}, u32[]{:S(2)}) collective-permute-start(bf16[20,32,128]{2,1,0:T(8,128)(2,1)S(1)} %get-tuple-element.162), channel_id=1, source_target_pairs={{0,24},{8,16},{16,8},{24,0},{1,25},{9,17},{17,9},{25,1},{2,26},{10... | collective-permute-start | bytes 491528 | tf_op jit(solution)/shard_map/cond/branch_2_fun/ppermute | solution.py:223
  28.0 0.7 copy-start.17
  28.6 32.5 %collective-permute-start.30 = (bf16[28,32,128]{2,1,0:T(8,128)(2,1)S(1)}, bf16[28,32,128]{2,1,0:T(8,128)(2,1)S(1)}, u32[]{:S(2)}, u32[]{:S(2)}) collective-permute-start(bf16[28,32,128]{2,1,0:T(8,128)(2,1)S(1)} %get-tuple-element.156), channel_id=1, source_target_pairs={{0,8},{8,0},{16,24},{24,16},{1,9},{9,1},{17,25},{25,17},{2,10},{10... | collective-permute-start | bytes 688136 | tf_op jit(solution)/shard_map/cond/branch_2_fun/ppermute | solution.py:223
  28.6 21.4 %collective-permute-start.31 = (bf16[20,32,128]{2,1,0:T(8,128)(2,1)}, bf16[20,32,128]{2,1,0:T(8,128)(2,1)}, u32[]{:S(2)}, u32[]{:S(2)}) collective-permute-start(bf16[20,32,128]{2,1,0:T(8,128)(2,1)} %get-tuple-element.157), channel_id=1, source_target_pairs={{0,16},{8,24},{16,0},{24,8},{1,17},{9,25},{17,1},{25,9},{2,18},{10... | collective-permute-start | bytes 491528 | tf_op jit(solution)/shard_map/cond/branch_2_fun/ppermute | solution.py:223
  35.8 15.8 %collective-permute-start.32 = (bf16[20,32,128]{2,1,0:T(8,128)(2,1)}, bf16[20,32,128]{2,1,0:T(8,128)(2,1)}, u32[]{:S(2)}, u32[]{:S(2)}) collective-permute-start(bf16[20,32,128]{2,1,0:T(8,128)(2,1)} %get-tuple-element.158), channel_id=1, source_target_pairs={{0,24},{8,16},{16,8},{24,0},{1,25},{9,17},{17,9},{25,1},{2,26},{10... | collective-permute-start | bytes 491528 | tf_op jit(solution)/shard_map/cond/branch_2_fun/ppermute | solution.py:223
  36.7 35.8 %collective-permute-start.27 = (bf16[28,32,128]{2,1,0:T(8,128)(2,1)S(1)}, bf16[28,32,128]{2,1,0:T(8,128)(2,1)S(1)}, u32[]{:S(2)}, u32[]{:S(2)}) collective-permute-start(bf16[28,32,128]{2,1,0:T(8,128)(2,1)S(1)} %get-tuple-element.152), channel_id=1, source_target_pairs={{0,8},{8,0},{16,24},{24,16},{1,9},{9,1},{17,25},{25,17},{2,10},{10... | collective-permute-start | bytes 688136 | tf_op jit(solution)/shard_map/cond/branch_2_fun/ppermute | solution.py:223
  41.3 24.7 %collective-permute-start.28 = (bf16[20,32,128]{2,1,0:T(8,128)(2,1)}, bf16[20,32,128]{2,1,0:T(8,128)(2,1)}, u32[]{:S(2)}, u32[]{:S(2)}) collective-permute-start(bf16[20,32,128]{2,1,0:T(8,128)(2,1)} %get-tuple-element.153), channel_id=1, source_target_pairs={{0,16},{8,24},{16,0},{24,8},{1,17},{9,25},{17,1},{25,9},{2,18},{10... | collective-permute-start | bytes 491528 | tf_op jit(solution)/shard_map/cond/branch_2_fun/ppermute | solution.py:223
  44.2 23.8 %all-to-all-start.11 = ((bf16[8,16,32,128]{3,2,1,0:T(8,128)(2,1)}), bf16[8,16,32,128]{3,2,1,0:T(8,128)(2,1)S(1)}, u32[]{:S(2)}, u32[]{:S(2)}) async-start(bf16[8,16,32,128]{3,2,1,0:T(8,128)(2,1)} %product.31), calls=%async_computation.11 | async-start | bytes 2097152 | tf_op jit(solution)/shard_map/cond/branch_2_fun/all_to_all | solution.py:238
  50.1 22.5 %collective-permute-start.29 = (bf16[20,32,128]{2,1,0:T(8,128)(2,1)}, bf16[20,32,128]{2,1,0:T(8,128)(2,1)}, u32[]{:S(2)}, u32[]{:S(2)}) collective-permute-start(bf16[20,32,128]{2,1,0:T(8,128)(2,1)} %get-tuple-element.154), channel_id=1, source_target_pairs={{0,24},{8,16},{16,8},{24,0},{1,25},{9,17},{17,9},{25,1},{2,26},{10... | collective-permute-start | bytes 491528 | tf_op jit(solution)/shard_map/cond/branch_2_fun/ppermute | solution.py:223
  51.7 39.8 %collective-permute-start.24 = (bf16[28,32,128]{2,1,0:T(8,128)(2,1)S(1)}, bf16[28,32,128]{2,1,0:T(8,128)(2,1)S(1)}, u32[]{:S(2)}, u32[]{:S(2)}) collective-permute-start(bf16[28,32,128]{2,1,0:T(8,128)(2,1)S(1)} %get-tuple-element.148), channel_id=1, source_target_pairs={{0,8},{8,0},{16,24},{24,16},{1,9},{9,1},{17,25},{25,17},{2,10},{10... | collective-permute-start | bytes 688136 | tf_op jit(solution)/shard_map/cond/branch_2_fun/ppermute | solution.py:223
  61.2 30.3 %collective-permute-start.25 = (bf16[20,32,128]{2,1,0:T(8,128)(2,1)}, bf16[20,32,128]{2,1,0:T(8,128)(2,1)S(1)}, u32[]{:S(2)}, u32[]{:S(2)}) collective-permute-start(bf16[20,32,128]{2,1,0:T(8,128)(2,1)} %copy-done.17), channel_id=1, source_target_pairs={{0,16},{8,24},{16,0},{24,8},{1,17},{9,25},{17,1},{25,9},{2,18},{10... | collective-permute-start | bytes 491528 | tf_op jit(solution)/shard_map/cond/branch_2_fun/ppermute | solution.py:223
  66.0 25.4 %collective-permute-start.26 = (bf16[20,32,128]{2,1,0:T(8,128)(2,1)S(1)}, bf16[20,32,128]{2,1,0:T(8,128)(2,1)S(1)}, u32[]{:S(2)}, u32[]{:S(2)}) collective-permute-start(bf16[20,32,128]{2,1,0:T(8,128)(2,1)S(1)} %get-tuple-element.150), channel_id=1, source_target_pairs={{0,24},{8,16},{16,8},{24,0},{1,25},{9,17},{17,9},{25,1},{2,26},{10... | collective-permute-start | bytes 491528 | tf_op jit(solution)/shard_map/cond/branch_2_fun/ppermute | solution.py:223
  68.0 1.0 copy-start.2
  69.0 18.9 %all-to-all-start.10 = ((bf16[8,16,32,128]{3,2,1,0:T(8,128)(2,1)}), bf16[8,16,32,128]{3,2,1,0:T(8,128)(2,1)S(1)}, u32[]{:S(2)}, u32[]{:S(2)}) async-start(bf16[8,16,32,128]{3,2,1,0:T(8,128)(2,1)} %product.30), calls=%async_computation.10 | async-start | bytes 2097152 | tf_op jit(solution)/shard_map/cond/branch_2_fun/all_to_all | solution.py:238
  87.9 18.9 %all-to-all-start.9 = ((bf16[8,16,32,128]{3,2,1,0:T(8,128)(2,1)}), bf16[8,16,32,128]{3,2,1,0:T(8,128)(2,1)S(1)}, u32[]{:S(2)}, u32[]{:S(2)}) async-start(bf16[8,16,32,128]{3,2,1,0:T(8,128)(2,1)} %product.29), calls=%async_computation.9 | async-start | bytes 2097152 | tf_op jit(solution)/shard_map/cond/branch_2_fun/all_to_all | solution.py:238
  94.4 1.0 copy-start.10
  106.8 18.9 %all-to-all-start.8 = ((bf16[8,16,32,128]{3,2,1,0:T(8,128)(2,1)}), bf16[8,16,32,128]{3,2,1,0:T(8,128)(2,1)S(1)}, u32[]{:S(2)}, u32[]{:S(2)}) async-start(bf16[8,16,32,128]{3,2,1,0:T(8,128)(2,1)} %copy-done.10), calls=%async_computation.8 | async-start | bytes 2097152 | tf_op jit(solution)/shard_map/cond/branch_2_fun/all_to_all | solution.py:238
  110.4 1.2 copy-start.3
  111.6 3.1 %copy-start.23 = (bf16[128,8192]{1,0:T(8,128)(2,1)S(1)}, bf16[128,8192]{1,0:T(8,128)(2,1)}, u32[]{:S(2)}) copy-start(bf16[128,8192]{1,0:T(8,128)(2,1)} %get-tuple-element.253.refs_1_) | copy-start | bytes 6291460 | tf_op jit(solution)/shard_map/cond
where the time goes:
time: 130 us; the launch traced here: 129 us
  waiting for transfers between devices  46.7 us (36%)
  starting transfers between devices  45.4 us (35%)
  Pallas kernels  31.1 us (24%)
  local copies, waits for them, and re-layouts  3.88 us (3%)
    all_to_all x4, waiting for transfers between devices, exchange(): sums = lax.all_to_all(sums, 'col', 0, 0, tiled=True)  30 us
    ppermute x12, starting transfers between devices, exchange(): lax.ppermute(packs[t], 'row', pairs(n_row, t))  23.8 us
    all_to_all x4, starting transfers between devices, exchange(): sums = lax.all_to_all(sums, 'col', 0, 0, tiled=True)  14.2 us
    pallas_call x4, Pallas kernels, exchange(): pl.pallas_call(lambda *refs: product_kernel(n_row, base, group, *refs), o...  13.7 us
    pallas_call x4, Pallas kernels, exchange(): pl.pallas_call(lambda *refs, first=first: combine_kernel(blk, first, chun...  9.72 us
    ppermute x12, waiting for transfers between devices, exchange(): lax.ppermute(packs[t], 'row', pairs(n_row, t))  9.56 us
    all_to_all x1, starting transfers between devices, body(): heard = lax.all_to_all(line, ('row', 'col'), 0, 0, tiled=True)  7.3 us
    all_to_all x1, waiting for transfers between devices, body(): heard = lax.all_to_all(line, ('row', 'col'), 0, 0, tiled=True)  7.07 us
  transfers between devices with their start and end apart: 17, of which 7 were waited for; matrix products, arithmetic and copies ran while one was open for 0% of the time, Pallas kernels for 18%

commit v1 on v0

--- a/solution.py
+++ b/solution.py
@@ -5,8 +5,8 @@
 from jax.experimental.pallas import tpu as pltpu
 from jax.sharding import PartitionSpec as P
 
-LEVELS = ((28, 16, 14), (28, 18, 14), (28, 20, 16), (32, 24, 20))
-PARTS = (32, 32, 32, 32)
+LEVELS = ((28, 18, 11), (28, 18, 12), (28, 20, 13), (28, 20, 14), (32, 24, 18))
+PARTS = (32, 48, 48)
 SHIFT = 1024
 COST = 1 << 16
 HIDE = 30_000_000_000
@@ -26,6 +26,10 @@
 
 def pairs(n, t):
     return [(i, i ^ t) for i in range(n)]
+
+
+def turns(n):
+    return [t for t in range(n) if t < 3] + [t for t in range(n - 1, 2, -1)]
 
 
 def number(index, per_piece, owner_of, n_owner, wide):
@@ -100,13 +104,15 @@
 
 
 def pack_kernel(n_row, n_col, blk, spans, heard, slab, *refs):
-    packs, (asks, sems) = refs[: n_row * len(spans)], refs[n_row * len(spans) :]
+    packs, (asks, held, sems) = refs[: n_row * len(spans)], refs[n_row * len(spans) :]
     row, col = lax.axis_index("row"), lax.axis_index("col")
+    start = spans[0][0]
     fetch(
         [
             pltpu.make_async_copy(heard.at[(row ^ t) * n_col + col], asks.at[t], sems.at[t])
             for t in range(n_row)
         ]
+        + [pltpu.make_async_copy(slab.at[pl.ds(start, held.shape[0])], held, sems.at[n_row])]
     )
     for p, (first, rows) in enumerate(spans):
         for t in range(n_row):
@@ -114,16 +120,15 @@
 
             def copy(i, carry):
                 at = pl.multiple_of((asks[t, 0, 1 + i] & (SHIFT - 1)) * blk, blk)
-                pack[i] = slab[first : first + rows, pl.ds(at, blk)]
+                pack[i] = held[first - start : first - start + rows, pl.ds(at, blk)]
                 return carry
 
             lax.fori_loop(0, asks[t, 0, 0] & (SHIFT - 1), copy, 0)
 
 
-def product_kernel(n_row, base, group, places, stored, *refs):
-    panels = refs[:n_row]
-    sums, held, total = refs[-3:]
-    n_col, cap = sums.shape[:2]
+def product_kernel(n_row, n_col, cap, base, group, places, stored, *refs):
+    panels, sums, (held, total) = refs[:n_row], refs[n_row:-2], refs[-2:]
+    turn = lax.axis_index("col") if len(sums) > 1 else 0
     for t, panel in enumerate(panels):
         held[base[t] : base[t] + panel.shape[0]] = panel[...]
     live = places[5, 0]
@@ -142,28 +147,34 @@
             products.append(jnp.dot(held[here], stored[s], preferred_element_type=jnp.float32))
         for u in range(group):
             s = g * group + u
-            o = jnp.where(s < live, places[2, s] * cap + places[3, s], n_col * cap)
+            o = jnp.where(s < live, (places[2, s] ^ turn) * cap + places[3, s], n_col * cap)
             total[o] = jnp.where(places[4, s] == 1, 0.0, total[o]) + products[u]
         return carry
 
     lax.fori_loop(0, lax.div(live + group - 1, group), step, 0)
     for t in range(n_col):
-        sums[t] = total[t * cap : (t + 1) * cap].astype(jnp.bfloat16)
-
-
-def combine_kernel(blk, first, chunks, lists, slab, sums, *refs):
-    out, total, ready, sems = refs[-4:]
-    n_col = sums.shape[0]
+        values = total[t * cap : (t + 1) * cap].astype(jnp.bfloat16)
+        if len(sums) > 1:
+            sums[turns(n_col).index(t)][...] = values
+        else:
+            sums[0][t] = values
+
+
+def combine_kernel(n_col, n_sums, blk, first, chunks, lists, slab, *refs):
+    sums, (out, total, ready, sems) = refs[:n_sums], refs[-4:]
+    turn = lax.axis_index("col") if n_sums > 1 else 0
     pieces, rows = total.shape[:2]
     for i in range(pieces):
         total[i] = 3.0 * slab[first : first + rows, i * blk : (i + 1) * blk].astype(jnp.float32)
     for t in range(n_col):
+        source = turns(n_col)[t] ^ turn if n_sums > 1 else t
+        here = sums[t] if n_sums > 1 else sums[0].at[t]
 
         def add(i, carry):
-            total[lists[t, 1 + i] >> 10] -= 2.0 * sums[t, i].astype(jnp.float32)
+            total[lists[source, 1 + i] >> 10] -= 2.0 * here[i].astype(jnp.float32)
             return carry
 
-        lax.fori_loop(0, lists[t, 0] >> 10, add, 0)
+        lax.fori_loop(0, lists[source, 0] >> 10, add, 0)
     each = pieces // chunks
     copies = []
     for q in range(chunks):
@@ -201,11 +212,12 @@
                 for first, rows in some
                 for c in caps_in
             ],
-            in_specs=[anywhere(), vmem()],
+            in_specs=[anywhere(), anywhere()],
             out_specs=[vmem()] * (n_row * len(some)),
             scratch_shapes=[
                 pltpu.SMEM((n_row,) + heard.shape[1:], jnp.int32),
-                pltpu.SemaphoreType.DMA((n_row,)),
+                pltpu.VMEM((sum(rows for first, rows in some), width), jnp.bfloat16),
+                pltpu.SemaphoreType.DMA((n_row + 1,)),
             ],
             compiler_params=params,
             cost_estimate=cost,
@@ -219,14 +231,17 @@
         places, packed[1:] = lax.optimization_barrier((places, packed[1:]))
     result = None
     for (first, rows), packs in zip(spans, packed):
+        last = len(spans) > 1 and first + rows == blk
         panels = [packs[0]] + [
             lax.ppermute(packs[t], "row", pairs(n_row, t)) for t in range(1, n_row)
         ]
         sums = pl.pallas_call(
-            lambda *refs: product_kernel(n_row, base, group, *refs),
-            out_shape=jax.ShapeDtypeStruct((n_col, cap, rows, blk), jnp.bfloat16),
+            lambda *refs: product_kernel(n_row, n_col, cap, base, group, *refs),
+            out_shape=[jax.ShapeDtypeStruct((cap, rows, blk), jnp.bfloat16)] * n_col
+            if last
+            else [jax.ShapeDtypeStruct((n_col, cap, rows, blk), jnp.bfloat16)],
             in_specs=[smem()] + [vmem()] * (1 + n_row),
-            out_specs=vmem(),
+            out_specs=[vmem()] * (n_col if last else 1),
             scratch_shapes=[
                 pltpu.VMEM((sum(caps_in), rows, blk), jnp.bfloat16),
                 pltpu.VMEM((n_col * cap + 1, rows, blk), jnp.float32),
@@ -235,23 +250,30 @@
             cost_estimate=pl.CostEstimate(flops=HIDE, bytes_accessed=COST, transcendentals=0),
             name="product",
         )(places, stored, *panels)
-        sums = lax.all_to_all(sums, "col", 0, 0, tiled=True)
+        if last:
+            sums = [sums[0]] + [
+                lax.ppermute(sums[i], "col", pairs(n_col, t))
+                for i, t in enumerate(turns(n_col))
+                if i > 0
+            ]
+        else:
+            sums = [lax.all_to_all(sums[0], "col", 0, 0, tiled=True)]
         extra = [] if result is None else [result]
         result = pl.pallas_call(
-            lambda *refs, first=first: combine_kernel(blk, first, chunks, *refs),
+            lambda *refs, first=first, n=len(sums): combine_kernel(n_col, n, blk, first, chunks, *refs),
             out_shape=jax.ShapeDtypeStruct(s_slab.shape, s_slab.dtype),
-            in_specs=[smem(), vmem(), vmem()] + [anywhere()] * len(extra),
+            in_specs=[smem()] + [vmem()] * (1 + len(sums)) + [anywhere()] * len(extra),
             out_specs=anywhere(),
             scratch_shapes=[
                 pltpu.VMEM((pieces, rows, blk), jnp.float32),
                 pltpu.VMEM((rows, width), jnp.bfloat16),
                 pltpu.SemaphoreType.DMA((chunks,)),
             ],
-            input_output_aliases={3: 0} if extra else {},
+            input_output_aliases={2 + len(sums): 0} if extra else {},
             compiler_params=params,
             cost_estimate=cost,
             name="combine",
-        )(lists, s_slab, sums, *extra)
+        )(lists, s_slab, *sums, *extra)
     return result
 
 

time: 130 us -> 96.1 us (0.74)
  the two profiles are of different devices: /device:TPU:0 before, /device:TPU:9 now
where the time goes in v1:
time: 96.1 us; the launch traced here: 94.6 us
  starting transfers between devices  38.7 us (40%)
  waiting for transfers between devices  31 us (32%)
  Pallas kernels  22.3 us (23%)
    ppermute x9, waiting for transfers between devices, exchange(): lax.ppermute(packs[t], 'row', pairs(n_row, t))  21.9 us
    all_to_all x2, starting transfers between devices, exchange(): sums = [lax.all_to_all(sums[0], 'col', 0, 0, tiled=True)]  14.3 us
    ppermute x9, starting transfers between devices, exchange(): lax.ppermute(packs[t], 'row', pairs(n_row, t))  9.12 us
    ppermute x7, starting transfers between devices, exchange(): lax.ppermute(sums[i], 'col', pairs(n_col, t))  8.96 us
    pallas_call x3, Pallas kernels, exchange(): pl.pallas_call(lambda *refs: product_kernel(n_row, n_col, cap, base, grou...  8.88 us
    pallas_call x3, Pallas kernels, exchange(): pl.pallas_call(lambda *refs, first=first, n=len(sums): combine_kernel(n_c...  7.79 us
    all_to_all x1, starting transfers between devices, body(): heard = lax.all_to_all(line, ('row', 'col'), 0, 0, tiled=True)  6.36 us
    all_to_all x1, waiting for transfers between devices, body(): heard = lax.all_to_all(line, ('row', 'col'), 0, 0, tiled=True)  5.46 us
  transfers between devices with their start and end apart: 19, of which 7 were waited for; matrix products, arithmetic and copies ran while one was open for 1% of the time, Pallas kernels for 18%

profile of v1, /device:TPU:9, one launch (start us, length us, event | category | flops | bytes accessed | tf_op | source)
XLA Modules:
  0.0 94.6 jit_solution(10968861863569948234)
XLA Ops:
  0.0 1.7 %ask.1 = (s32[32,128]{1,0:T(8,128)}, s32[6,64]{1,0:T(8,128)S(1)}) custom-call(s32[1,1,2,64]{3,2,1,0:T(2,128)} %refs_0_.1), custom_call_target="tpu_custom_call" | custom-call | tf_op jit(solution)/shard_map/ask/pallas_call | solution.py:293
  1.7 6.4 %all-to-all-start.12 = ((s32[32,1,128]{2,1,0:T(1,128)}), s32[32,1,128]{2,1,0:T(1,128)S(1)}, u32[]{:S(2)}, u32[]{:S(2)}) async-start(s32[32,1,128]{2,1,0:T(1,128)} %bitcast.47), calls=%async_computation.12 | async-start | bytes 32768 | tf_op jit(solution)/shard_map/all_to_all | solution.py:301
  8.0 5.5 %all-to-all-done.12 = s32[32,1,128]{2,1,0:T(1,128)S(1)} async-done(((s32[32,1,128]{2,1,0:T(1,128)}), s32[32,1,128]{2,1,0:T(1,128)S(1)}, u32[]{:S(2)}, u32[]{:S(2)}) %all-to-all-start.12) | async-done | bytes 16416 | tf_op jit(solution)/shard_map/all_to_all | solution.py:301
  14.9 79.6 %conditional.1 = (bf16[128,8192]{1,0:T(8,128)(2,1)}) conditional(s32[]{:T(128)} %clamp.3, (s32[32,1,128]{2,1,0:T(1,128)S(1)}, bf16[128,8192]{1,0:T(8,128)(2,1)}, s32[6,64]{1,0:T(8,128)S(1)}, bf16[1,1,64,128,128]{4,3,2,1,0:T(8,128)(2,1)}, s32[32,1,128]{2,1,0:T(1,128)S(1)}, /*index=5*/s32[]{:T(128)}, s32[]{:T(128)}, ...), branch_computations={%region_1.0_spmd, %region_2.0_spmd, %region_3.0_spmd, %region_4.0_... | conditional | flops 89999998976 | bytes 126428200 | solution.py:312
  14.9 1.6 %pack.13 = (bf16[28,32,128]{2,1,0:T(8,128)(2,1)S(1)}, bf16[28,32,128]{2,1,0:T(8,128)(2,1)S(1)}, bf16[18,32,128]{2,1,0:T(8,128)(2,1)S(1)}, bf16[18,32,128]{2,1,0:T(8,128)(2,1)S(1)}) custom-call(s32[32,1,128]{2,1,0:T(1,128)S(1)} %get-tuple-element.453, bf16[128,8192]{1,0:T(8,128)(2,1)} %get-tuple-element.299.refs_1_), custom_call_target="tpu_custom_call" | custom-call | bytes 65536 | tf_op jit(solution)/shard_map/cond/branch_0_fun/pack/pallas_call | solution.py:208
  19.3 2.3 %pack.12 = (bf16[28,48,128]{2,1,0:T(8,128)(2,1)S(1)}, bf16[28,48,128]{2,1,0:T(8,128)(2,1)S(1)}, bf16[18,48,128]{2,1,0:T(8,128)(2,1)}, bf16[18,48,128]{2,1,0:T(8,...) custom-call(s32[32,1,128]{2,1,0:T(1,128)S(1)} %get-tuple-element.453, ...), custom_call_target="tpu_custom_call" | custom-call | bytes 65536 | tf_op jit(solution)/shard_map/cond/branch_0_fun/pack/pallas_call | solution.py:208
  21.6 2.3 %collective-permute-start.10 = (bf16[28,48,128]{2,1,0:T(8,128)(2,1)S(1)}, bf16[28,48,128]{2,1,0:T(8,128)(2,1)S(1)}, u32[]{:S(2)}, u32[]{:S(2)}) collective-permute-start(bf16[28,48,128]{2,1,0:T(8,128)(2,1)S(1)} %get-tuple-element.99), channel_id=1, source_target_pairs={{0,8},{8,0},{16,24},{24,16},{1,9},{9,1},{17,25},{25,17},{2,10},{10... | collective-permute-start | bytes 1032200 | tf_op jit(solution)/shard_map/cond/branch_0_fun/ppermute | solution.py:236
  23.9 2.4 %collective-permute-done.14.refs_4_ = bf16[18,32,128]{2,1,0:T(8,128)(2,1)S(1)} collective-permute-done((bf16[18,32,128]{2,1,0:T(8,128)(2,1)S(1)}, bf16[18,32,128]{2,1,0:T(8,128)(2,1)S(1)}, u32[]{:S(2)}, u32[]{:S(2)}) %collective-permute-start.14) | collective-permute-done | bytes 147488 | tf_op jit(solution)/shard_map/cond/branch_0_fun/ppermute | solution.py:236
  27.5 4.4 %collective-permute-done.15.refs_5_ = bf16[18,32,128]{2,1,0:T(8,128)(2,1)S(1)} collective-permute-done((bf16[18,32,128]{2,1,0:T(8,128)(2,1)S(1)}, bf16[18,32,128]{2,1,0:T(8,128)(2,1)S(1)}, u32[]{:S(2)}, u32[]{:S(2)}) %collective-permute-start.15) | collective-permute-done | bytes 147488 | tf_op jit(solution)/shard_map/cond/branch_0_fun/ppermute | solution.py:236
  32.5 2.1 %product.20 = bf16[8,11,32,128]{3,2,1,0:T(8,128)(2,1)} custom-call(s32[6,64]{1,0:T(8,128)S(1)} %get-tuple-element.84.refs_0_, bf16[64,128,128]{2,1,0:T(8,128)(2,1)S(1)} %bitcast.50, bf16[28,32,128]{2,1,0:T(8,128)(2,1)S(1)} %get-tuple-element.102.refs_2_, bf16[28,32,128]{2,1,0:T(8,128)(2,1)S(1)} %collective-permute-done.13.refs_3_, ...), custom_call_target="tpu_custom_call" | custom-call | flops 30000001024 | bytes 65536 | tf_op jit(solution)/shard_map/cond/branch_0_fun/product/pallas_call | solution.py:238
  34.7 7.8 %all-to-all-start.1 = ((bf16[8,11,32,128]{3,2,1,0:T(8,128)(2,1)}), bf16[8,11,32,128]{3,2,1,0:T(8,128)(2,1)S(1)}, u32[]{:S(2)}, u32[]{:S(2)}) async-start(bf16[8,11,32,128]{3,2,1,0:T(8,128)(2,1)} %product.20), calls=%async_computation.1 | async-start | bytes 1441792 | tf_op jit(solution)/shard_map/cond/branch_0_fun/all_to_all | solution.py:260
  42.5 2.3 %collective-permute-start.2 = (bf16[18,48,128]{2,1,0:T(8,128)(2,1)S(1)}, bf16[18,48,128]{2,1,0:T(8,128)(2,1)}, u32[]{:S(2)}, u32[]{:S(2)}) collective-permute-start(bf16[18,48,128]{2,1,0:T(8,128)(2,1)S(1)} %get-tuple-element.89), channel_id=1, source_target_pairs={{0,24},{8,16},{16,8},{24,0},{1,25},{9,17},{17,9},{25,1},{2,26},{10... | collective-permute-start | bytes 663560 | tf_op jit(solution)/shard_map/cond/branch_0_fun/ppermute | solution.py:236
  44.8 6.2 %collective-permute-done.12.refs_5_ = bf16[18,48,128]{2,1,0:T(8,128)(2,1)} collective-permute-done((bf16[18,48,128]{2,1,0:T(8,128)(2,1)}, bf16[18,48,128]{2,1,0:T(8,128)(2,1)}, u32[]{:S(2)}, u32[]{:S(2)}) %collective-permute-start.12) | collective-permute-done | bytes 221216 | tf_op jit(solution)/shard_map/cond/branch_0_fun/ppermute | solution.py:236
  50.9 3.5 %product.19 = bf16[8,11,48,128]{3,2,1,0:T(8,128)(2,1)} custom-call(s32[6,64]{1,0:T(8,128)S(1)} %get-tuple-element.84.refs_0_, bf16[64,128,128]{2,1,0:T(8,128)(2,1)} %bitcast.48, bf16[28,48,128]{2,1,0:T(8,128)(2,1)S(1)} %get-tuple-element.98.refs_2_, bf16[28,48,128]{2,1,0:T(8,128)(2,1)S(1)} %collective-permute-done.10.refs_3_, ...), custom_call_target="tpu_custom_call" | custom-call | flops 30000001024 | bytes 65536 | tf_op jit(solution)/shard_map/cond/branch_0_fun/product/pallas_call | solution.py:238
  54.5 6.4 %all-to-all-start = ((bf16[8,11,48,128]{3,2,1,0:T(8,128)(2,1)}), bf16[8,11,48,128]{3,2,1,0:T(8,128)(2,1)S(1)}, u32[]{:S(2)}, u32[]{:S(2)}) async-start(bf16[8,11,48,128]{3,2,1,0:T(8,128)(2,1)} %product.19), calls=%async_computation | async-start | bytes 2162688 | tf_op jit(solution)/shard_map/cond/branch_0_fun/all_to_all | solution.py:260
  60.9 9.0 %collective-permute-done.2.refs_5_ = bf16[18,48,128]{2,1,0:T(8,128)(2,1)} collective-permute-done((bf16[18,48,128]{2,1,0:T(8,128)(2,1)S(1)}, bf16[18,48,128]{2,1,0:T(8,128)(2,1)}, u32[]{:S(2)}, u32[]{:S(2)}) %collective-permute-start.2) | collective-permute-done | bytes 221216 | tf_op jit(solution)/shard_map/cond/branch_0_fun/ppermute | solution.py:236
  69.9 3.2 %product.18 = (bf16[11,48,128]{2,1,0:T(8,128)(2,1)S(1)}, bf16[11,48,128]{2,1,0:T(8,128)(2,1)S(1)}, bf16[11,48,128]{2,1,0:T(8,128)(2,1)S(1)}, bf16[11,48,128]{2,1...) custom-call(s32[6,64]{1,0:T(8,128)S(1)} %get-tuple-element.84.refs_0, ...), custom_call_target="tpu_custom_call" | custom-call | flops 30000001024 | bytes 65536 | tf_op jit(solution)/shard_map/cond/branch_0_fun/product/pallas_call | solution.py:238
  73.1 1.6 %collective-permute-start.3 = (bf16[11,48,128]{2,1,0:T(8,128)(2,1)S(1)}, bf16[11,48,128]{2,1,0:T(8,128)(2,1)S(1)}, u32[]{:S(2)}, u32[]{:S(2)}) collective-permute-start(bf16[11,48,128]{2,1,0:T(8,128)(2,1)S(1)} %get-tuple-element.91), channel_id=1, source_target_pairs={{0,1},{1,0},{2,3},{3,2},{4,5},{5,4},{6,7},{7,6},{8,9},{9,8},{10,11... | collective-permute-start | bytes 405512 | tf_op jit(solution)/shard_map/cond/branch_0_fun/ppermute | solution.py:255
  76.7 1.6 %collective-permute-start.6 = (bf16[11,48,128]{2,1,0:T(8,128)(2,1)}, bf16[11,48,128]{2,1,0:T(8,128)(2,1)S(1)}, u32[]{:S(2)}, u32[]{:S(2)}) collective-permute-start(bf16[11,48,128]{2,1,0:T(8,128)(2,1)} %get-tuple-element.94), channel_id=1, source_target_pairs={{0,6},{1,7},{2,4},{3,5},{4,2},{5,3},{6,0},{7,1},{8,14},{9,15},{10,... | collective-permute-start | bytes 405512 | tf_op jit(solution)/shard_map/cond/branch_0_fun/ppermute | solution.py:255
  80.2 1.9 %collective-permute-start.9 = (bf16[11,48,128]{2,1,0:T(8,128)(2,1)S(1)}, bf16[11,48,128]{2,1,0:T(8,128)(2,1)S(1)}, u32[]{:S(2)}, u32[]{:S(2)}) collective-permute-start(bf16[11,48,128]{2,1,0:T(8,128)(2,1)S(1)} %get-tuple-element.97), channel_id=1, source_target_pairs={{0,3},{1,2},{2,1},{3,0},{4,7},{5,6},{6,5},{7,4},{8,11},{9,10},{10,... | collective-permute-start | bytes 405512 | tf_op jit(solution)/shard_map/cond/branch_0_fun/ppermute | solution.py:255
  82.7 2.8 %combine.18.refs_3_ = bf16[128,8192]{1,0:T(8,128)(2,1)} custom-call(s32[8,128]{1,0:T(8,128)S(1)} %dynamic-slice_bitcast_fusion.refs_0_, bf16[128,8192]{1,0:T(8,128)(2,1)} %get-tuple-element.299.refs_1_, bf16[8,11,32,128]{3,2,1,0:T(8,128)(2,1)S(1)} %all-to-all-done.1.refs_2_), custom_call_target="tpu_custom_call" | custom-call | bytes 65536 | tf_op jit(solution)/shard_map/cond/branch_0_fun/combine/pallas_call | solution.py:262
  85.5 3.1 %combine.19.refs_10_ = bf16[128,8192]{1,0:T(8,128)(2,1)} custom-call(s32[8,128]{1,0:T(8,128)S(1)} %dynamic-slice_bitcast_fusion.refs_0_, bf16[128,8192]{1,0:T(8,128)(2,1)} %get-tuple-element.299.refs_1_, bf16[8,11,48,128]{3,2,1,0:T(8,128)(2,1)S(1)} %all-to-all-done.refs_2_, bf16[128,8192]{1,0:T(8,128)(2,1)} %combine.18.refs_3_), custom_call_target="tpu_custom_call", output_to_operand_aliasing={{}: (3, {})} | custom-call | bytes 65536 | tf_op jit(solution)/shard_map/cond/branch_0_fun/combine/pallas_call | solution.py:262
  89.4 2.9 %collective-permute-done.8.refs_8_ = bf16[11,48,128]{2,1,0:T(8,128)(2,1)S(1)} collective-permute-done((bf16[11,48,128]{2,1,0:T(8,128)(2,1)S(1)}, bf16[11,48,128]{2,1,0:T(8,128)(2,1)S(1)}, u32[]{:S(2)}, u32[]{:S(2)}) %collective-permute-start.8) | collective-permute-done | bytes 135200 | tf_op jit(solution)/shard_map/cond/branch_0_fun/ppermute | solution.py:255
  92.3 1.9 %combine.20 = bf16[128,8192]{1,0:T(8,128)(2,1)} custom-call(s32[8,128]{1,0:T(8,128)S(1)} %dynamic-slice_bitcast_fusion.refs_0_, bf16[128,8192]{1,0:T(8,128)(2,1)S(1)} %copy-done.10, bf16[11,48,128]{2,1,0:T(8,128)(2,1)S(1)} %get-tuple-element.90.refs_2_, bf16[11,48,128]{2,1,0:T(8,128)(2,1)S(1)} %collective-permute-done.3.refs_3_, ...), custom_call_target="tpu_custom_call", output_to_operand_aliasing={{}: (10, {})} | custom-call | bytes 65536 | tf_op jit(solution)/shard_map/cond/branch_0_fun/combine/pallas_call | solution.py:262
  (34 shorter events, 10.7 us)
Async XLA Ops:
  1.7 11.8 %all-to-all-start.12 = ((s32[32,1,128]{2,1,0:T(1,128)}), s32[32,1,128]{2,1,0:T(1,128)S(1)}, u32[]{:S(2)}, u32[]{:S(2)}) async-start(s32[32,1,128]{2,1,0:T(1,128)} %bitcast.47), calls=%async_computation.12 | async-start | bytes 32768 | tf_op jit(solution)/shard_map/all_to_all | solution.py:301
  14.9 12.6 %copy-start.21 = (s32[32,1,128]{2,1,0:T(1,128)}, s32[32,1,128]{2,1,0:T(1,128)S(1)}, u32[]{:S(2)}) copy-start(s32[32,1,128]{2,1,0:T(1,128)S(1)} %get-tuple-element.453) | copy-start | bytes 49156 | tf_op jit(solution)/shard_map/cond
  14.9 4.4 %copy-start.9 = (bf16[128,8192]{1,0:T(8,128)(2,1)S(1)}, bf16[128,8192]{1,0:T(8,128)(2,1)}, u32[]{:S(2)}) copy-start(bf16[128,8192]{1,0:T(8,128)(2,1)} %get-tuple-element.299.refs_1_) | copy-start | bytes 6291460 | tf_op jit(solution)/shard_map/cond
  14.9 17.6 %copy-start.28 = (bf16[1,1,64,128,128]{4,3,2,1,0:T(8,128)(2,1)S(1)}, bf16[1,1,64,128,128]{4,3,2,1,0:T(8,128)(2,1)}, u32[]{:S(2)}) copy-start(bf16[1,1,64,128,128]{4,3,2,1,0:T(8,128)(2,1)} %get-tuple-element.329) | copy-start | bytes 6291460 | tf_op jit(solution)/shard_map/cond
  16.6 15.3 %collective-permute-start.13 = (bf16[28,32,128]{2,1,0:T(8,128)(2,1)S(1)}, bf16[28,32,128]{2,1,0:T(8,128)(2,1)S(1)}, u32[]{:S(2)}, u32[]{:S(2)}) collective-permute-start(bf16[28,32,128]{2,1,0:T(8,128)(2,1)S(1)} %get-tuple-element.103), channel_id=1, source_target_pairs={{0,8},{8,0},{16,24},{24,16},{1,9},{9,1},{17,25},{25,17},{2,10},{10... | collective-permute-start | bytes 688136 | tf_op jit(solution)/shard_map/cond/branch_0_fun/ppermute | solution.py:236
  17.9 8.4 %collective-permute-start.14 = (bf16[18,32,128]{2,1,0:T(8,128)(2,1)S(1)}, bf16[18,32,128]{2,1,0:T(8,128)(2,1)S(1)}, u32[]{:S(2)}, u32[]{:S(2)}) collective-permute-start(bf16[18,32,128]{2,1,0:T(8,128)(2,1)S(1)} %get-tuple-element.104), channel_id=1, source_target_pairs={{0,16},{8,24},{16,0},{24,8},{1,17},{9,25},{17,1},{25,9},{2,18},{10... | collective-permute-start | bytes 442376 | tf_op jit(solution)/shard_map/cond/branch_0_fun/ppermute | solution.py:236
  18.1 13.7 %collective-permute-start.15 = (bf16[18,32,128]{2,1,0:T(8,128)(2,1)S(1)}, bf16[18,32,128]{2,1,0:T(8,128)(2,1)S(1)}, u32[]{:S(2)}, u32[]{:S(2)}) collective-permute-start(bf16[18,32,128]{2,1,0:T(8,128)(2,1)S(1)} %get-tuple-element.105), channel_id=1, source_target_pairs={{0,24},{8,16},{16,8},{24,0},{1,25},{9,17},{17,9},{25,1},{2,26},{10... | collective-permute-start | bytes 442376 | tf_op jit(solution)/shard_map/cond/branch_0_fun/ppermute | solution.py:236
  21.6 29.3 %collective-permute-start.10 = (bf16[28,48,128]{2,1,0:T(8,128)(2,1)S(1)}, bf16[28,48,128]{2,1,0:T(8,128)(2,1)S(1)}, u32[]{:S(2)}, u32[]{:S(2)}) collective-permute-start(bf16[28,48,128]{2,1,0:T(8,128)(2,1)S(1)} %get-tuple-element.99), channel_id=1, source_target_pairs={{0,8},{8,0},{16,24},{24,16},{1,9},{9,1},{17,25},{25,17},{2,10},{10... | collective-permute-start | bytes 1032200 | tf_op jit(solution)/shard_map/cond/branch_0_fun/ppermute | solution.py:236
  23.9 18.6 %collective-permute-start.11 = (bf16[18,48,128]{2,1,0:T(8,128)(2,1)}, bf16[18,48,128]{2,1,0:T(8,128)(2,1)}, u32[]{:S(2)}, u32[]{:S(2)}) collective-permute-start(bf16[18,48,128]{2,1,0:T(8,128)(2,1)} %get-tuple-element.100), channel_id=1, source_target_pairs={{0,16},{8,24},{16,0},{24,8},{1,17},{9,25},{17,1},{25,9},{2,18},{10... | collective-permute-start | bytes 663560 | tf_op jit(solution)/shard_map/cond/branch_0_fun/ppermute | solution.py:236
  26.3 24.6 %collective-permute-start.12 = (bf16[18,48,128]{2,1,0:T(8,128)(2,1)}, bf16[18,48,128]{2,1,0:T(8,128)(2,1)}, u32[]{:S(2)}, u32[]{:S(2)}) collective-permute-start(bf16[18,48,128]{2,1,0:T(8,128)(2,1)} %get-tuple-element.101), channel_id=1, source_target_pairs={{0,24},{8,16},{16,8},{24,0},{1,25},{9,17},{17,9},{25,1},{2,26},{10... | collective-permute-start | bytes 663560 | tf_op jit(solution)/shard_map/cond/branch_0_fun/ppermute | solution.py:236
  31.8 38.1 %collective-permute-start = (bf16[28,48,128]{2,1,0:T(8,128)(2,1)S(1)}, bf16[28,48,128]{2,1,0:T(8,128)(2,1)S(1)}, u32[]{:S(2)}, u32[]{:S(2)}) collective-permute-start(bf16[28,48,128]{2,1,0:T(8,128)(2,1)S(1)} %get-tuple-element.87), channel_id=1, source_target_pairs={{0,8},{8,0},{16,24},{24,16},{1,9},{9,1},{17,25},{25,17},{2,10},{10... | collective-permute-start | bytes 1032200 | tf_op jit(solution)/shard_map/cond/branch_0_fun/ppermute | solution.py:236
  31.8 29.1 %collective-permute-start.1 = (bf16[18,48,128]{2,1,0:T(8,128)(2,1)S(1)}, bf16[18,48,128]{2,1,0:T(8,128)(2,1)}, u32[]{:S(2)}, u32[]{:S(2)}) collective-permute-start(bf16[18,48,128]{2,1,0:T(8,128)(2,1)S(1)} %get-tuple-element.88), channel_id=1, source_target_pairs={{0,16},{8,24},{16,0},{24,8},{1,17},{9,25},{17,1},{25,9},{2,18},{10... | collective-permute-start | bytes 663560 | tf_op jit(solution)/shard_map/cond/branch_0_fun/ppermute | solution.py:236
  34.7 19.8 %all-to-all-start.1 = ((bf16[8,11,32,128]{3,2,1,0:T(8,128)(2,1)}), bf16[8,11,32,128]{3,2,1,0:T(8,128)(2,1)S(1)}, u32[]{:S(2)}, u32[]{:S(2)}) async-start(bf16[8,11,32,128]{3,2,1,0:T(8,128)(2,1)} %product.20), calls=%async_computation.1 | async-start | bytes 1441792 | tf_op jit(solution)/shard_map/cond/branch_0_fun/all_to_all | solution.py:260
  42.5 27.4 %collective-permute-start.2 = (bf16[18,48,128]{2,1,0:T(8,128)(2,1)S(1)}, bf16[18,48,128]{2,1,0:T(8,128)(2,1)}, u32[]{:S(2)}, u32[]{:S(2)}) collective-permute-start(bf16[18,48,128]{2,1,0:T(8,128)(2,1)S(1)} %get-tuple-element.89), channel_id=1, source_target_pairs={{0,24},{8,16},{16,8},{24,0},{1,25},{9,17},{17,9},{25,1},{2,26},{10... | collective-permute-start | bytes 663560 | tf_op jit(solution)/shard_map/cond/branch_0_fun/ppermute | solution.py:236
  54.5 31.0 %all-to-all-start = ((bf16[8,11,48,128]{3,2,1,0:T(8,128)(2,1)}), bf16[8,11,48,128]{3,2,1,0:T(8,128)(2,1)S(1)}, u32[]{:S(2)}, u32[]{:S(2)}) async-start(bf16[8,11,48,128]{3,2,1,0:T(8,128)(2,1)} %product.19), calls=%async_computation | async-start | bytes 2162688 | tf_op jit(solution)/shard_map/cond/branch_0_fun/all_to_all | solution.py:260
  73.1 6.1 %collective-permute-start.3 = (bf16[11,48,128]{2,1,0:T(8,128)(2,1)S(1)}, bf16[11,48,128]{2,1,0:T(8,128)(2,1)S(1)}, u32[]{:S(2)}, u32[]{:S(2)}) collective-permute-start(bf16[11,48,128]{2,1,0:T(8,128)(2,1)S(1)} %get-tuple-element.91), channel_id=1, source_target_pairs={{0,1},{1,0},{2,3},{3,2},{4,5},{5,4},{6,7},{7,6},{8,9},{9,8},{10,11... | collective-permute-start | bytes 405512 | tf_op jit(solution)/shard_map/cond/branch_0_fun/ppermute | solution.py:255
  74.7 5.5 %collective-permute-start.4 = (bf16[11,48,128]{2,1,0:T(8,128)(2,1)S(1)}, bf16[11,48,128]{2,1,0:T(8,128)(2,1)S(1)}, u32[]{:S(2)}, u32[]{:S(2)}) collective-permute-start(bf16[11,48,128]{2,1,0:T(8,128)(2,1)S(1)} %get-tuple-element.92), channel_id=1, source_target_pairs={{0,2},{1,3},{2,0},{3,1},{4,6},{5,7},{6,4},{7,5},{8,10},{9,11},{10,... | collective-permute-start | bytes 405512 | tf_op jit(solution)/shard_map/cond/branch_0_fun/ppermute | solution.py:255
  75.8 12.8 %collective-permute-start.5 = (bf16[11,48,128]{2,1,0:T(8,128)(2,1)}, bf16[11,48,128]{2,1,0:T(8,128)(2,1)S(1)}, u32[]{:S(2)}, u32[]{:S(2)}) collective-permute-start(bf16[11,48,128]{2,1,0:T(8,128)(2,1)} %get-tuple-element.93), channel_id=1, source_target_pairs={{0,7},{1,6},{2,5},{3,4},{4,3},{5,2},{6,1},{7,0},{8,15},{9,14},{10,... | collective-permute-start | bytes 405512 | tf_op jit(solution)/shard_map/cond/branch_0_fun/ppermute | solution.py:255
  76.7 11.9 %collective-permute-start.6 = (bf16[11,48,128]{2,1,0:T(8,128)(2,1)}, bf16[11,48,128]{2,1,0:T(8,128)(2,1)S(1)}, u32[]{:S(2)}, u32[]{:S(2)}) collective-permute-start(bf16[11,48,128]{2,1,0:T(8,128)(2,1)} %get-tuple-element.94), channel_id=1, source_target_pairs={{0,6},{1,7},{2,4},{3,5},{4,2},{5,3},{6,0},{7,1},{8,14},{9,15},{10,... | collective-permute-start | bytes 405512 | tf_op jit(solution)/shard_map/cond/branch_0_fun/ppermute | solution.py:255
  78.3 11.1 %collective-permute-start.7 = (bf16[11,48,128]{2,1,0:T(8,128)(2,1)S(1)}, bf16[11,48,128]{2,1,0:T(8,128)(2,1)S(1)}, u32[]{:S(2)}, u32[]{:S(2)}) collective-permute-start(bf16[11,48,128]{2,1,0:T(8,128)(2,1)S(1)} %get-tuple-element.95), channel_id=1, source_target_pairs={{0,5},{1,4},{2,7},{3,6},{4,1},{5,0},{6,3},{7,2},{8,13},{9,12},{10,... | collective-permute-start | bytes 405512 | tf_op jit(solution)/shard_map/cond/branch_0_fun/ppermute | solution.py:255
  79.2 13.1 %collective-permute-start.8 = (bf16[11,48,128]{2,1,0:T(8,128)(2,1)S(1)}, bf16[11,48,128]{2,1,0:T(8,128)(2,1)S(1)}, u32[]{:S(2)}, u32[]{:S(2)}) collective-permute-start(bf16[11,48,128]{2,1,0:T(8,128)(2,1)S(1)} %get-tuple-element.96), channel_id=1, source_target_pairs={{0,4},{1,5},{2,6},{3,7},{4,0},{5,1},{6,2},{7,3},{8,12},{9,13},{10,... | collective-permute-start | bytes 405512 | tf_op jit(solution)/shard_map/cond/branch_0_fun/ppermute | solution.py:255
  80.2 12.1 %collective-permute-start.9 = (bf16[11,48,128]{2,1,0:T(8,128)(2,1)S(1)}, bf16[11,48,128]{2,1,0:T(8,128)(2,1)S(1)}, u32[]{:S(2)}, u32[]{:S(2)}) collective-permute-start(bf16[11,48,128]{2,1,0:T(8,128)(2,1)S(1)} %get-tuple-element.97), channel_id=1, source_target_pairs={{0,3},{1,2},{2,1},{3,0},{4,7},{5,6},{6,5},{7,4},{8,11},{9,10},{10,... | collective-permute-start | bytes 405512 | tf_op jit(solution)/shard_map/cond/branch_0_fun/ppermute | solution.py:255
  85.5 6.8 %copy-start.10 = (bf16[128,8192]{1,0:T(8,128)(2,1)S(1)}, bf16[128,8192]{1,0:T(8,128)(2,1)}, u32[]{:S(2)}) copy-start(bf16[128,8192]{1,0:T(8,128)(2,1)} %get-tuple-element.299.refs_1_) | copy-start | bytes 6291460 | tf_op jit(solution)/shard_map/cond
